TPU v7x, 512 devices: a whole 4x4x16 slice. The times are simulated.
512 devices in a mesh: rep: 16 (over z_lo, core), shard: 32 (over z_hi, y, x).
Axes of the slice: x: 4, y: 4, z: 16 (z_hi: 2, z_lo: 8; z = z_hi * 8 + z_lo), core: 2. Of those that a mesh axis runs over, the one named last changes fastest.
Arguments:
- layer_input: bfloat16 [65536, 8192], P(('rep', 'shard')), may hold values from -24 to 24
- queries: bfloat16 [65536, 512], P(('rep', 'shard')), may hold values from -10 to 10
- d_out: bfloat16 [65536, 512], P(('rep', 'shard')), may hold values from -6 to 6
- segment_ids: int32 [512, 128], P(('rep', 'shard')), may hold values from 0 to 3, never falling along the last dimension, each value on 1 to 64 neighbouring positions
- kv_weight: bfloat16 [8192, 256], P('shard'), may hold values from -0.0625 to 0.0625
Outputs:
- d_input: bfloat16 [65536, 8192], P(('rep', 'shard'))
- d_queries: bfloat16 [65536, 512], P(('rep', 'shard'))
- d_kv_weight: float32 [8192, 256], P('shard')
All inputs are finite; a program needn't handle non-finite values.
Results may differ from a plain program's by a relative error of at most 0.03.
Values may be sent and summed in bfloat16 or wider, within the bound.
A program may use at most 64 MiB of HBM per device.

v0:
```python
import jax
import jax.numpy as jnp
from jax import lax
from jax.sharding import PartitionSpec as P

HEAD = 128
QH = 4


def attention_grad(queries, keyval, d_out, segment):
    rows = queries.shape[0]
    scale = 1.0 / HEAD**0.5
    heads = queries.reshape(rows, QH, HEAD)
    grads = d_out.reshape(rows, QH, HEAD)
    keys = keyval[:, :HEAD]
    values = keyval[:, HEAD:]
    position = jnp.arange(rows)
    allowed = (segment[:, None] == segment[None, :]) & (position[None, :] <= position[:, None])
    scores = jnp.einsum("thd,sd->hts", heads, keys, preferred_element_type=jnp.float32) * scale
    scores = jnp.where(allowed[None], scores, -1e30)
    top = jnp.max(scores, axis=2, keepdims=True)
    weights = jnp.where(allowed[None], jnp.exp(scores - top), 0.0)
    probs = weights / jnp.sum(weights, axis=2, keepdims=True)
    probs_low = probs.astype(jnp.bfloat16)
    attended = jnp.einsum("hts,sd->thd", probs_low, values, preferred_element_type=jnp.float32)
    delta = jnp.sum(grads.astype(jnp.float32) * attended, axis=2)
    dprob = jnp.einsum("thd,sd->hts", grads, values, preferred_element_type=jnp.float32)
    dscore = (probs * (dprob - jnp.transpose(delta)[:, :, None])).astype(jnp.bfloat16)
    d_queries = (
        jnp.einsum("hts,sd->thd", dscore, keys, preferred_element_type=jnp.float32) * scale
    ).astype(jnp.bfloat16)
    d_keys = jnp.einsum("hts,thd->sd", dscore, heads, preferred_element_type=jnp.float32) * scale
    d_values = jnp.einsum("hts,thd->sd", probs_low, grads, preferred_element_type=jnp.float32)
    d_keyval = jnp.concatenate([d_keys, d_values], axis=1).astype(jnp.bfloat16)
    return (d_queries.reshape(rows, QH * HEAD), d_keyval)


def transposed_product(left, right):
    return lax.dot_general(
        left, right, (((1,), (1,)), ((), ())), preferred_element_type=jnp.float32
    )


def body(layer_input, queries, d_out, segment_ids, kv_weight):
    columns = layer_input
    keyval = jnp.dot(
        columns,
        lax.all_gather(kv_weight, "shard", axis=0, tiled=True),
        preferred_element_type=jnp.float32,
    ).astype(jnp.bfloat16)
    d_queries, d_keyval = attention_grad(queries, keyval, d_out, segment_ids[0])
    d_input = transposed_product(d_keyval, lax.all_gather(kv_weight, "shard", axis=0, tiled=True))
    columns = layer_input
    owned = lax.psum_scatter(
        lax.dot_general(
            columns, d_keyval, (((0,), (0,)), ((), ())), preferred_element_type=jnp.float32
        ).astype(jnp.bfloat16),
        "shard",
        scatter_dimension=0,
        tiled=True,
    ).astype(jnp.float32)
    d_kv_weight = lax.psum(owned, "rep")
    return (d_input.astype(jnp.bfloat16), d_queries, d_kv_weight)


def solution(mesh):
    return jax.shard_map(
        body,
        mesh=mesh,
        in_specs=(
            P(("rep", "shard"), None),
            P(("rep", "shard"), None),
            P(("rep", "shard"), None),
            P(("rep", "shard"), None),
            P("shard", None),
        ),
        out_specs=(P(("rep", "shard"), None), P(("rep", "shard"), None), P("shard", None)),
        check_vma=False,
    )
```

profile of v0, /device:TPU:1, one launch (start us, length us, event | category | flops | bytes accessed | tf_op | source)
XLA Modules:
  0.0 751.3 jit_solution(8471183318444992419)
XLA Ops:
  7.2 0.0 copy-start
  7.2 0.0 all-gather.2.cloned.1.call-start
  7.2 0.7 all-gather.2.cloned.1.call-update
  7.9 0.0 reduce-scatter.2.cloned.1.call-start
  8.0 1.0 copy.29
  9.0 1.0 copy.9
  10.0 0.8 fusion.17
  10.8 167.2 %all-gather.2.cloned.1.call-done = bf16[8192,256]{1,0:T(8,128)(2,1)} async-done(((bf16[256,256]{1,0:T(8,128)(2,1)}), bf16[8192,256]{1,0:T(8,128)(2,1)}) %all-gather.2.cloned.1.call-update) | async-done | bytes 4194320 | tf_op jit(solution)/shard_map/all_gather | solution.py:48
  178.1 0.0 copy-done
  178.1 2.9 convolution_convert_fusion.2
  181.0 0.2 fusion.25
  181.2 0.2 fusion.12
  181.5 0.2 fusion.15
  181.7 0.2 fusion.10
  181.8 0.2 fusion.14
  182.0 3.2 fusion.1
  185.3 0.0 reduce-scatter.2.cloned.1.call-update
  185.3 0.2 fusion.11
  185.5 0.8 copy.18
  186.3 5.0 convolution_convert_fusion.1
  191.3 451.0 %reduce-scatter.2.cloned.1.call-done = bf16[256,256]{0,1:T(8,128)(2,1)} async-done(((bf16[8192,256]{0,1:T(8,128)(2,1)}), bf16[256,256]{0,1:T(8,128)(2,1)}) %reduce-scatter.2.cloned.1.call-update) | async-done | bytes 131088 | tf_op jit(solution)/shard_map/reduce_scatter | solution.py:54
  642.2 101.4 %all-reduce.1 = f32[256,256]{0,1:T(8,128)S(1)} all-reduce(bf16[256,256]{0,1:T(8,128)(2,1)} %reduce-scatter.2.cloned.1.call-done), channel_id=1, replica_groups=mesh['rep'=16,'shard'=32] {'rep'}, use_global_device_ids=true, to_apply=%region_4.5 | all-reduce | flops 65536 | bytes 393216 | tf_op jit(solution)/shard_map/psum | solution.py:62
  743.6 0.8 copy.19
Async XLA Ops:
  7.2 170.9 %copy-start = (bf16[128,8192]{1,0:T(8,128)(2,1)S(1)}, bf16[128,8192]{1,0:T(8,128)(2,1)}, u32[]{:S(2)}) copy-start(bf16[128,8192]{1,0:T(8,128)(2,1)} %param.5) | copy-start | bytes 6291460
  7.2 170.9 %all-gather.2.cloned.1.call-start = ((), (), s32[]{:S(2)}) async-start(), calls=%async_computation.1 | async-start | bytes 4325376 | tf_op jit(solution)/shard_map/all_gather | solution.py:48
  7.9 634.3 %reduce-scatter.2.cloned.1.call-start = ((), (), s32[]{:S(2)}) async-start(), calls=%async_computation.2 | async-start | bytes 4325376 | tf_op jit(solution)/shard_map/reduce_scatter | solution.py:54
Sparse Core Ops, SparseCore 0:
  12.3 165.7 all-gather.1
  185.4 456.8 reduce-scatter.1
where the time goes:
time: 754 us; the launch traced here: 751 us
  waiting for transfers between devices  619 us (82%)
  blocking collectives  101 us (13%)
  between operations  14.1 us (2%)
  matrix products  12.4 us (2%)
    reduce_scatter x1, waiting for transfers between devices, body(): lax.psum_scatter(lax.dot_general(columns, d_keyval, (((0,), (0,)), ((), (...  451 us
    all_gather x1, waiting for transfers between devices, body(): lax.all_gather(kv_weight, 'shard', axis=0, tiled=True)  167 us
    psum x1, blocking collectives, body(): d_kv_weight = lax.psum(owned, 'rep')  101 us
  transfers between devices with their start and end apart: 2, of which 2 were waited for; matrix products, arithmetic and copies ran while one was open for 1% of the time, Pallas kernels for 0%

commit v1 on v0

v1 whole, which is shorter than its diff:
```python
import jax
import jax.numpy as jnp
from jax import lax
from jax.experimental import pallas as pl
from jax.experimental.pallas import tpu as pltpu
from jax.sharding import PartitionSpec as P

HEAD = 128
QH = 4
SCALE = 1.0 / HEAD**0.5
BF16 = jnp.bfloat16
F32 = jnp.float32
MESH = pl.DeviceIdType.MESH


def dot(a, b):
    return jnp.dot(a, b, preferred_element_type=F32)


def dot_nt(a, b):
    return lax.dot_general(a, b, (((1,), (1,)), ((), ())), preferred_element_type=F32)


def dot_tn(a, b):
    return lax.dot_general(a, b, (((0,), (0,)), ((), ())), preferred_element_type=F32)


def shard_at(zh, outer, inner, core):
    y = outer * (1 - core) + inner * core
    x = inner * (1 - core) + outer * core
    return zh * 16 + y * 4 + x


def kernel(
    x_ref, q_ref, g_ref, seg_ref, w_ref,
    dx_ref, dq_ref, dw_ref,
    xb, xt, wb, qv, gv, segv, mask, part, part_in, dst, dkv, di, dqv,
    far, to_right, to_left, far_l, far_r, in_l, in_r,
    inner_out, inner_in, z_out, z_in, fin, fin_in, dwv,
    local, x_send, x_recv, w_send, w_recv, p2_send, p2_recv, m_send, m_recv,
    c_send, c_recv, dx_send, dx_recv, r1_send, r1_recv, r2_send, r2_recv,
    z_send, z_recv, f_send, f_recv,
):
    rep, shard = lax.axis_index("rep"), lax.axis_index("shard")
    core, zl = rep % 2, rep // 2
    zh, y, x = shard // 16, (shard // 4) % 4, shard % 4
    outer = y * (1 - core) + x * core
    inner = x * (1 - core) + y * core
    right, left, across = (outer + 1) % 4, (outer + 3) % 4, (outer + 2) % 4

    def on_outer(o):
        return (rep, shard_at(zh, o, inner, core))

    def on_inner(i):
        return (rep, shard_at(zh, outer, i, core))

    def on_z(half, low):
        return (low * 2 + core, shard_at(half, outer, inner, core))

    partner = (zl * 2 + 1 - core, shard)
    mirror = on_z(1 - zh, 7 - zl)

    def rows128(i):
        return pl.ds(pl.multiple_of(i * 128, 128), 128)

    def remote(src, dst_, ssem, rsem, device):
        return pltpu.make_async_remote_copy(
            src_ref=src, dst_ref=dst_, send_sem=ssem, recv_sem=rsem,
            device_id=device, device_id_type=MESH,
        )

    def arrived(ref, sem):
        pltpu.make_async_copy(ref, ref, sem).wait()

    pending = []

    def send(src, dst_, ssem, rsem, device):
        copy = remote(src, dst_, ssem, rsem, device)
        copy.start()
        pending.append(copy)

    barrier = pltpu.get_barrier_semaphore()
    friends = [partner, on_outer(right), on_outer(left)]
    friends += [on_inner((inner + d) % 4) for d in (1, 2, 3)]
    friends += [on_z(zh, (zl + d) % 8) for d in range(1, 8)]
    friends += [on_z(1 - zh, (zl + d) % 8) for d in range(8)]
    for friend in friends:
        pl.semaphore_signal(barrier, inc=1, device_id=friend, device_id_type=MESH)

    own_w = w_ref.at[rows128(core), :]
    w_here = pltpu.make_async_copy(own_w, wb.at[0, outer, rows128(inner), :], local.at[0])
    w_here.start()
    loads = [
        pltpu.make_async_copy(q_ref, qv, local.at[1]),
        pltpu.make_async_copy(g_ref, gv, local.at[2]),
        pltpu.make_async_copy(seg_ref, segv, local.at[3]),
    ]
    for load in loads:
        load.start()

    def x_columns(n, for_core):
        k, i = n // 4, n % 4
        half, o = (k // 4 + zh) % 2, k % 4
        column = shard_at(half, o, i, for_core) * 256 + for_core * 128
        return k, pl.ds(pl.multiple_of(i * 128, 128), 128), pl.ds(pl.multiple_of(column, 128), 128)

    def load_x(n, _):
        k, to, frm = x_columns(n, core)
        pltpu.make_async_copy(
            x_ref.at[:, frm], xb.at[k, pl.ds(0, 128), to], local.at[4]
        ).start()
        return 0

    lax.fori_loop(0, 32, load_x, 0)
    pl.semaphore_wait(barrier, len(friends))

    for d in (1, 3, 2):
        send(own_w, wb.at[0, outer, rows128(inner), :], w_send.at[0, d - 1], w_recv.at[0, d - 1],
             on_inner((inner + d) % 4))
    send(own_w, wb.at[1, outer, rows128(inner), :], m_send, m_recv, mirror)

    def send_x(n, _):
        k, to, frm = x_columns(n, 1 - core)
        remote(
            x_ref.at[:, frm], xb.at[k, pl.ds(128, 128), to], x_send, x_recv, partner
        ).start()
        return 0

    lax.fori_loop(0, 32, send_x, 0)

    top, bottom = pl.ds(0, 256), pl.ds(256, 256)

    def first_ring_done(h):
        for d in (1, 3, 2):
            arrived(wb.at[h, outer, rows128((inner - d + 4) % 4), :], w_recv.at[h, d - 1])

    def second_ring(h):
        def go(part_, slot, device):
            block = wb.at[h, outer, part_, :]
            send(block, block, p2_send.at[h, slot], p2_recv.at[h, slot], device)

        go(top, 0, on_outer(right))
        go(bottom, 2, on_outer(left))
        go(bottom, 1, on_outer(right))
        go(top, 3, on_outer(left))

    def relay(h):
        block = wb.at[h, left, top, :]
        arrived(block, p2_recv.at[h, 0])
        send(block, block, p2_send.at[h, 4], p2_recv.at[h, 4], on_outer(right))
        block = wb.at[h, right, bottom, :]
        arrived(block, p2_recv.at[h, 2])
        send(block, block, p2_send.at[h, 5], p2_recv.at[h, 5], on_outer(left))

    def add_block(h, o):
        part[...] += dot(xb[h * 4 + o], wb[h, o])

    def turn(h, o):
        xt[h * 4 + o] = xb[h * 4 + o].T

    w_here.wait()
    first_ring_done(0)
    second_ring(0)

    part[...] = jnp.zeros_like(part)
    for load in loads:
        load.wait()
    across_lanes = jnp.broadcast_to(segv[...], (128, 128))
    same = across_lanes.T == across_lanes
    row = lax.broadcasted_iota(jnp.int32, (128, 128), 0)
    column = lax.broadcasted_iota(jnp.int32, (128, 128), 1)
    mask[...] = jnp.where(same & (row <= column), 0.0, -1e30)

    relay(0)
    arrived(wb.at[1, outer, rows128(inner), :], m_recv)
    mirrored = wb.at[1, outer, rows128(inner), :]
    for d in (1, 3, 2):
        send(mirrored, mirrored, w_send.at[1, d - 1], w_recv.at[1, d - 1],
             on_inner((inner + d) % 4))
    arrived(xb.at[pl.ds(0, 4)], local.at[4])
    arrived(xb.at[pl.ds(0, 4)], x_recv)
    add_block(0, outer)
    first_ring_done(1)
    second_ring(1)
    for n in range(4):
        turn(0, n)
    arrived(wb.at[0, left, bottom, :], p2_recv.at[0, 1])
    add_block(0, left)
    arrived(wb.at[0, right, top, :], p2_recv.at[0, 3])
    add_block(0, right)
    relay(1)
    arrived(wb.at[0, across, top, :], p2_recv.at[0, 4])
    arrived(wb.at[0, across, bottom, :], p2_recv.at[0, 5])
    add_block(0, across)
    add_block(1, outer)
    for n in range(4):
        turn(1, n)
    arrived(wb.at[1, left, bottom, :], p2_recv.at[1, 1])
    add_block(1, left)
    arrived(wb.at[1, right, top, :], p2_recv.at[1, 3])
    add_block(1, right)
    arrived(wb.at[1, across, top, :], p2_recv.at[1, 4])
    arrived(wb.at[1, across, bottom, :], p2_recv.at[1, 5])
    add_block(1, across)

    send(part.at[pl.ds(128, 128), :], part_in, c_send.at[0], c_recv.at[0], partner)
    arrived(part_in, c_recv.at[0])
    keyval = (part[pl.ds(0, 128), :] + part_in[...]).astype(BF16)
    keys, values = keyval[:, :HEAD], keyval[:, HEAD:]

    d_keys = jnp.zeros((128, HEAD), F32)
    d_values = jnp.zeros((128, HEAD), F32)
    for n in range(QH):
        cols = pl.ds(n * HEAD, HEAD)
        q, g = qv[:, cols], gv[:, cols]
        scores = dot_nt(keys, q) * SCALE + mask[...]
        weights = jnp.exp(scores - jnp.max(scores, axis=0, keepdims=True))
        probs = weights * (1.0 / jnp.sum(weights, axis=0, keepdims=True))
        d_probs = dot_nt(values, g)
        low = probs.astype(BF16)
        delta = jnp.sum(low.astype(F32) * d_probs, axis=0, keepdims=True)
        d_score = (probs * (d_probs - delta)).astype(BF16)
        dst[:, cols] = d_score
        d_keys += dot(d_score, q)
        d_values += dot(low, g)
    dkv[pl.ds(0, 128), pl.ds(0, HEAD)] = (d_keys * SCALE).astype(BF16)
    dkv[pl.ds(0, 128), pl.ds(HEAD, HEAD)] = d_values.astype(BF16)
    send(dkv.at[pl.ds(0, 128), :], dkv.at[pl.ds(128, 128), :], c_send.at[1], c_recv.at[1], partner)

    for n in range(QH):
        cols = pl.ds(n * HEAD, HEAD)
        dqv[:, cols] = (dot_tn(dst[:, cols], keys) * SCALE).astype(BF16)
    dq_out = pltpu.make_async_copy(dqv, dq_ref, local.at[5])
    dq_out.start()
    arrived(dkv.at[pl.ds(128, 128), :], c_recv.at[1])

    def term(h, o, rows):
        return dot(xt[h * 4 + o, rows, :], dkv[...])

    def send_far(h):
        far[h, top, :] = term(h, across, top).astype(BF16)
        send(far.at[h, top, :], far_l.at[h], r1_send.at[h, 0], r1_recv.at[h, 0], on_outer(right))
        far[h, bottom, :] = term(h, across, bottom).astype(BF16)
        send(far.at[h, bottom, :], far_r.at[h], r1_send.at[h, 1], r1_recv.at[h, 1], on_outer(left))

    def send_near(h):
        to_right[h, bottom, :] = term(h, right, bottom).astype(BF16)
        send(to_right.at[h, bottom, :], in_l.at[h, bottom, :], r1_send.at[h, 2], r1_recv.at[h, 2], on_outer(right))
        to_left[h, top, :] = term(h, left, top).astype(BF16)
        send(to_left.at[h, top, :], in_r.at[h, top, :], r1_send.at[h, 3], r1_recv.at[h, 3], on_outer(left))

    def send_joined(h):
        arrived(far_l.at[h], r1_recv.at[h, 0])
        to_right[h, top, :] = (term(h, right, top) + far_l[h].astype(F32)).astype(BF16)
        send(to_right.at[h, top, :], in_l.at[h, top, :], r1_send.at[h, 4], r1_recv.at[h, 4], on_outer(right))
        arrived(far_r.at[h], r1_recv.at[h, 1])
        to_left[h, bottom, :] = (term(h, left, bottom) + far_r[h].astype(F32)).astype(BF16)
        send(to_left.at[h, bottom, :], in_r.at[h, bottom, :], r1_send.at[h, 5], r1_recv.at[h, 5], on_outer(left))

    def input_grad(h, o):
        k = h * 4 + o
        di[k] = dot_nt(dkv[...], wb[h, o]).astype(BF16)

    def store_dx(n, _):
        k, frm, to = x_columns(n, core)
        pltpu.make_async_copy(
            di.at[k, pl.ds(0, 128), frm], dx_ref.at[:, to], local.at[6]
        ).start()
        remote(
            di.at[k, pl.ds(128, 128), frm], dx_ref.at[:, to], dx_send, dx_recv, partner
        ).start()
        return 0

    send_far(0)
    send_near(0)
    send_far(1)
    send_joined(0)
    send_near(1)
    send_joined(1)
    for n in range(4):
        input_grad(0, n)
    lax.fori_loop(0, 16, store_dx, 0)

    def outer_sum(h, i):
        rows = rows128(i)
        return term(h, outer, rows) + in_l[h, rows, :].astype(F32) + in_r[h, rows, :].astype(F32)

    def inner_ring(h):
        arrived(in_l.at[h, bottom, :], r1_recv.at[h, 2])
        arrived(in_r.at[h, top, :], r1_recv.at[h, 3])
        arrived(in_l.at[h, top, :], r1_recv.at[h, 4])
        arrived(in_r.at[h, bottom, :], r1_recv.at[h, 5])
        for d in (2, 1, 3):
            i = (inner + d) % 4
            inner_out[h, d - 1] = outer_sum(h, i).astype(BF16)
            send(inner_out.at[h, d - 1], inner_in.at[h, d - 1], r2_send.at[h, d - 1],
                 r2_recv.at[h, d - 1], on_inner(i))

    def plane_sum(h):
        total = outer_sum(h, inner)
        for d in (1, 3, 2):
            arrived(inner_in.at[h, d - 1], r2_recv.at[h, d - 1])
            total += inner_in[h, d - 1].astype(F32)
        z_out[h] = total.astype(BF16)
        for d in range(8):
            if h == 0 and d == 0:
                continue
            low = (zl + d) % 8
            rows = pl.ds(pl.multiple_of(low * 16, 16), 16)
            slot = h * 8 + d
            send(z_out.at[h, rows, :], z_in.at[slot], z_send.at[slot], z_recv.at[slot],
                 on_z((zh + h) % 2, low))

    inner_ring(0)
    for n in range(4):
        input_grad(1, n)
    plane_sum(0)
    lax.fori_loop(16, 32, store_dx, 0)
    inner_ring(1)
    plane_sum(1)

    mine = pl.ds(pl.multiple_of(zl * 16, 16), 16)
    total = z_out[0, mine, :].astype(F32)
    for slot in range(1, 16):
        arrived(z_in.at[slot], z_recv.at[slot])
        total += z_in[slot].astype(F32)
    fin[mine, :] = total.astype(BF16)
    for d in range(1, 8):
        send(fin.at[mine, :], fin.at[mine, :], f_send.at[d - 1], f_recv.at[d - 1],
             on_z(zh, (zl + d) % 8))
    for d in range(1, 8):
        rows = pl.ds(pl.multiple_of(((zl - d + 8) % 8) * 16, 16), 16)
        arrived(fin.at[rows, :], f_recv.at[d - 1])
    send(fin, fin_in, c_send.at[2], c_recv.at[2], partner)
    dwv[rows128(core), :] = fin[...].astype(F32)
    arrived(fin_in, c_recv.at[2])
    dwv[rows128(1 - core), :] = fin_in[...].astype(F32)
    dw_out = pltpu.make_async_copy(dwv, dw_ref, local.at[7])
    dw_out.start()

    for copy in pending:
        copy.wait_send()
    half_x = xb.at[pl.ds(0, 4)]
    arrived(half_x, x_send)
    arrived(half_x, dx_send)
    arrived(half_x, local.at[6])
    arrived(half_x, dx_recv)
    dq_out.wait()
    dw_out.wait()


def body(layer_input, queries, d_out, segment_ids, kv_weight):
    dma = pltpu.SemaphoreType.DMA
    any_space = pl.BlockSpec(memory_space=pl.ANY)
    return pl.pallas_call(
        kernel,
        out_shape=(
            jax.ShapeDtypeStruct((128, 8192), BF16),
            jax.ShapeDtypeStruct((128, 512), BF16),
            jax.ShapeDtypeStruct((256, 256), F32),
        ),
        in_specs=[any_space] * 5,
        out_specs=(any_space,) * 3,
        scratch_shapes=[
            pltpu.VMEM((8, 256, 512), BF16),
            pltpu.VMEM((8, 512, 256), BF16),
            pltpu.VMEM((2, 4, 512, 256), BF16),
            pltpu.VMEM((128, 512), BF16),
            pltpu.VMEM((128, 512), BF16),
            pltpu.VMEM((1, 128), jnp.int32),
            pltpu.VMEM((128, 128), F32),
            pltpu.VMEM((256, 256), F32),
            pltpu.VMEM((128, 256), F32),
            pltpu.VMEM((128, 512), BF16),
            pltpu.VMEM((256, 256), BF16),
            pltpu.VMEM((8, 256, 512), BF16),
            pltpu.VMEM((128, 512), BF16),
            pltpu.VMEM((2, 512, 256), BF16),
            pltpu.VMEM((2, 512, 256), BF16),
            pltpu.VMEM((2, 512, 256), BF16),
            pltpu.VMEM((2, 256, 256), BF16),
            pltpu.VMEM((2, 256, 256), BF16),
            pltpu.VMEM((2, 512, 256), BF16),
            pltpu.VMEM((2, 512, 256), BF16),
            pltpu.VMEM((2, 3, 128, 256), BF16),
            pltpu.VMEM((2, 3, 128, 256), BF16),
            pltpu.VMEM((2, 128, 256), BF16),
            pltpu.VMEM((16, 16, 256), BF16),
            pltpu.VMEM((128, 256), BF16),
            pltpu.VMEM((128, 256), BF16),
            pltpu.VMEM((256, 256), F32),
            dma((8,)),
            dma(()),
            dma(()),
            dma((2, 3)),
            dma((2, 3)),
            dma((2, 6)),
            dma((2, 6)),
            dma(()),
            dma(()),
            dma((3,)),
            dma((3,)),
            dma(()),
            dma(()),
            dma((2, 6)),
            dma((2, 6)),
            dma((2, 3)),
            dma((2, 3)),
            dma((16,)),
            dma((16,)),
            dma((7,)),
            dma((7,)),
        ],
        compiler_params=pltpu.CompilerParams(
            collective_id=0, has_side_effects=True, vmem_limit_bytes=40 * 1024 * 1024
        ),
    )(layer_input, queries, d_out, segment_ids, kv_weight)


def solution(mesh):
    return jax.shard_map(
        body,
        mesh=mesh,
        in_specs=(
            P(("rep", "shard"), None),
            P(("rep", "shard"), None),
            P(("rep", "shard"), None),
            P(("rep", "shard"), None),
            P("shard", None),
        ),
        out_specs=(P(("rep", "shard"), None), P(("rep", "shard"), None), P("shard", None)),
        check_vma=False,
    )
```

time: 754 us -> 88.7 us (0.12)
  waiting for transfers between devices: 619 us -> 0 us
  blocking collectives: 101 us -> 0 us
  Pallas kernels: 0 us -> 80.2 us
  between operations: 14.1 us -> 0.65 us
  matrix products: 12.4 us -> 0 us
    reduce_scatter x1 -> x0, waiting for transfers between devices: 451 us -> none  [body(): lax.psum_scatter(lax.dot_general(columns, d_keyval, (((0,), (0,)), ((), (...]
    all_gather x1 -> x0, waiting for transfers between devices: 167 us -> none  [body(): lax.all_gather(kv_weight, 'shard', axis=0, tiled=True)]
    psum x1 -> x0, blocking collectives: 101 us -> none  [body(): d_kv_weight = lax.psum(owned, 'rep')]
    pallas_call x0 -> x1, Pallas kernels: none -> 80.2 us  [body(): pl.pallas_call(kernel, out_shape=(jax.ShapeDtypeStruct((128, 8192), BF16)...]
    dot_general x8 -> x0, matrix products: 12.1 us -> none  [the longest x1 5.01 us: transposed_product(): lax.dot_general(left, right, (((1,), (1,)), ((), ())), preferred_element_...]
  transfers between devices with their start and end apart: 2 -> 0, of which waited for: 2 -> 0; matrix products, arithmetic and copies ran while one was open for 1% -> 0% of each run, Pallas kernels for 0% -> 0%
where the time goes in v1:
time: 88.7 us; the launch traced here: 88.5 us
  Pallas kernels  80.2 us (90%)
  local copies, waits for them, and re-layouts  7.63 us (9%)
    pallas_call x1, Pallas kernels, body(): pl.pallas_call(kernel, out_shape=(jax.ShapeDtypeStruct((128, 8192), BF16)...  80.2 us
    unnamed x13, local copies, waits for them, and re-layouts  7.63 us

profile of v1, /device:TPU:1, one launch (start us, length us, event | category | flops | bytes accessed | tf_op | source)
XLA Modules:
  0.0 88.5 jit_solution(3237847031714369205)
XLA Ops:
  0.6 0.0 copy-start
  0.6 1.6 %copy-done = bf16[128,8192]{1,0:T(8,128)(2,1)S(1)} copy-done((bf16[128,8192]{1,0:T(8,128)(2,1)S(1)}, bf16[128,8192]{1,0:T(8,128)(2,1)}, u32[]{:S(2)}) %copy-start) | copy-done | bytes 2097176
  2.2 0.0 copy-start.1
  2.2 0.9 %copy-done.1 = bf16[128,512]{1,0:T(8,128)(2,1)S(1)} copy-done((bf16[128,512]{1,0:T(8,128)(2,1)S(1)}, bf16[128,512]{1,0:T(8,128)(2,1)}, u32[]{:S(2)}) %copy-start.1) | copy-done | bytes 131096
  3.1 0.0 copy-start.2
  3.1 0.9 %copy-done.2 = bf16[128,512]{1,0:T(8,128)(2,1)S(1)} copy-done((bf16[128,512]{1,0:T(8,128)(2,1)S(1)}, bf16[128,512]{1,0:T(8,128)(2,1)}, u32[]{:S(2)}) %copy-start.2) | copy-done | bytes 131096
  4.0 0.0 copy-start.3
  4.0 0.9 %copy-done.3 = bf16[256,256]{1,0:T(8,128)(2,1)S(1)} copy-done((bf16[256,256]{1,0:T(8,128)(2,1)S(1)}, bf16[256,256]{1,0:T(8,128)(2,1)}, u32[]{:S(2)}) %copy-start.3) | copy-done | bytes 131096
  4.9 0.0 copy-start.4
  4.9 0.7 copy-done.4
  5.6 80.2 %shard_map.76 = (bf16[128,8192]{1,0:T(8,128)(2,1)S(1)}, bf16[128,512]{1,0:T(8,128)(2,1)S(1)}, f32[256,256]{1,0:T(8,128)S(1)}) custom-call(bf16[128,8192]{1,0:T(8,128)(2,1)S(1)} %copy-done, bf16[128,512]{1,0:T(8,128)(2,1)S(1)} %copy-done.1, bf16[128,512]{1,0:T(8,128)(2,1)S(1)} %copy-done.2, s32[1,128]{1,0:T(1,128)S(1)} %copy-done.4, ...), custom_call_target="tpu_custom_call" | custom-call | tf_op jit(solution)/shard_map/pallas_call | solution.py:355
  85.8 1.3 %copy.11 = bf16[128,8192]{1,0:T(8,128)(2,1)} copy(bf16[128,8192]{1,0:T(8,128)(2,1)S(1)} %get-tuple-element.6) | data formatting | bytes 4194304
  87.2 0.7 copy.12
  87.8 0.7 copy.13
Async XLA Ops:
  0.6 1.6 %copy-start = (bf16[128,8192]{1,0:T(8,128)(2,1)S(1)}, bf16[128,8192]{1,0:T(8,128)(2,1)}, u32[]{:S(2)}) copy-start(bf16[128,8192]{1,0:T(8,128)(2,1)} %x_ref.1) | copy-start | bytes 6291460
  2.2 0.9 %copy-start.1 = (bf16[128,512]{1,0:T(8,128)(2,1)S(1)}, bf16[128,512]{1,0:T(8,128)(2,1)}, u32[]{:S(2)}) copy-start(bf16[128,512]{1,0:T(8,128)(2,1)} %q_ref.1) | copy-start | bytes 393220
  3.1 0.9 %copy-start.2 = (bf16[128,512]{1,0:T(8,128)(2,1)S(1)}, bf16[128,512]{1,0:T(8,128)(2,1)}, u32[]{:S(2)}) copy-start(bf16[128,512]{1,0:T(8,128)(2,1)} %g_ref.1) | copy-start | bytes 393220
  4.0 0.9 %copy-start.3 = (bf16[256,256]{1,0:T(8,128)(2,1)S(1)}, bf16[256,256]{1,0:T(8,128)(2,1)}, u32[]{:S(2)}) copy-start(bf16[256,256]{1,0:T(8,128)(2,1)} %w_ref.1) | copy-start | bytes 393220
  4.9 0.7 copy-start.4

commit v2 on v1

v2 whole, which is shorter than its diff:
```python
import jax
import jax.numpy as jnp
from jax import lax
from jax.experimental import pallas as pl
from jax.experimental.pallas import tpu as pltpu
from jax.sharding import PartitionSpec as P

HEAD = 128
QH = 4
SCALE = 1.0 / HEAD**0.5
BF16 = jnp.bfloat16
F32 = jnp.float32
MESH = pl.DeviceIdType.MESH


def dot(a, b):
    return jnp.dot(a, b, preferred_element_type=F32)


def dot_nt(a, b):
    return lax.dot_general(a, b, (((1,), (1,)), ((), ())), preferred_element_type=F32)


def dot_tn(a, b):
    return lax.dot_general(a, b, (((0,), (0,)), ((), ())), preferred_element_type=F32)


def shard_at(zh, outer, inner, core):
    y = outer * (1 - core) + inner * core
    x = inner * (1 - core) + outer * core
    return zh * 16 + y * 4 + x


def kernel(
    x_ref, q_ref, g_ref, seg_ref, w_ref,
    dx_ref, dq_ref, dw_ref,
    xb, xt, wb, qv, gv, segv, mask, part, part_in, dst, dkv, di, dqv,
    far, joined, far_l, far_r, in_l, in_r,
    inner_out, inner_in, z_out, z_in, fin, fin_in, dwv,
    local, x_send, x_recv, w_send, w_recv, p2_send, p2_recv, m_send, m_recv,
    c_send, c_recv, dx_send, dx_recv, r1_send, r1_recv, r2_send, r2_recv,
    z_send, z_recv, f_send, f_recv, known,
):
    rep, shard = lax.axis_index("rep"), lax.axis_index("shard")
    core, zl = rep % 2, rep // 2
    zh, y, x = shard // 16, (shard // 4) % 4, shard % 4
    outer = y * (1 - core) + x * core
    inner = x * (1 - core) + y * core
    right, left, across = (outer + 1) % 4, (outer + 3) % 4, (outer + 2) % 4

    def on_outer(o):
        return (rep, shard_at(zh, o, inner, core))

    def on_inner(i):
        return (rep, shard_at(zh, outer, i, core))

    def on_z(half, low):
        return (low * 2 + core, shard_at(half, outer, inner, core))

    partner = (zl * 2 + 1 - core, shard)
    is_edge = (zl == 0) | (zl == 7)

    def on_z_at(d):
        z = (zh * 8 + zl + d + 16) % 16
        return on_z(z // 8, z % 8)


    def rows128(i):
        return pl.ds(pl.multiple_of(i * 128, 128), 128)

    def remote(src, dst_, ssem, rsem, device):
        return pltpu.make_async_remote_copy(
            src_ref=src, dst_ref=dst_, send_sem=ssem, recv_sem=rsem,
            device_id=device, device_id_type=MESH,
        )

    started = {}

    def sem_of(name):
        return name[0].at[name[1:]] if len(name) > 1 else name[0]

    def key_of(name):
        return (id(name[0]),) + name[1:]

    def finish():
        for ref, sem in list(started.values()):
            if callable(ref):
                ref()
                del started[key_of(sem)]
            else:
                arrived(ref, sem)

    def opened(ref, sem):
        started[key_of(sem)] = (ref, sem)

    def arrived(ref, sem):
        del started[key_of(sem)]
        pltpu.make_async_copy(ref, ref, sem_of(sem)).wait()

    def send(src, dst_, ssem, rsem, device):
        remote(src, dst_, sem_of(ssem), sem_of(rsem), device).start()
        opened(src, ssem)
        opened(dst_, rsem)

    def copy_here(src, dst_, sem):
        pltpu.make_async_copy(src, dst_, sem_of(sem)).start()
        opened(dst_, sem)

    barrier = pltpu.get_barrier_semaphore()
    friends = [partner, on_outer(right), on_outer(left)]
    friends += [on_inner((inner + d) % 4) for d in (1, 2, 3)]
    friends += [on_z_at(1), on_z_at(-1)]
    near = len(friends)
    friends.append(on_z(1 - zh, 7 * (1 - zl // 4)))
    for friend in friends:
        pl.semaphore_signal(barrier, inc=1, device_id=friend, device_id_type=MESH)

    own_w = w_ref.at[rows128(core), :]
    first_w = wb.at[0, outer, rows128(inner), :]
    copy_here(own_w, first_w, (local, 0))
    copy_here(q_ref, qv, (local, 1))
    copy_here(g_ref, gv, (local, 2))
    copy_here(seg_ref, segv, (local, 3))

    def x_columns(n, for_core):
        k, i = n // 4, n % 4
        half, o = (k // 4 + zh) % 2, k % 4
        column = shard_at(half, o, i, for_core) * 256 + for_core * 128
        return k, pl.ds(pl.multiple_of(i * 128, 128), 128), pl.ds(pl.multiple_of(column, 128), 128)

    def load_x(n, _):
        k, to, frm = x_columns(n, core)
        pltpu.make_async_copy(
            x_ref.at[:, frm], xb.at[k, pl.ds(0, 128), to], local.at[4]
        ).start()
        return 0

    half_x = xb.at[pl.ds(0, 4)]
    lax.fori_loop(0, 32, load_x, 0)
    opened(half_x, (local, 4))
    pl.semaphore_wait(barrier, near + 4 * is_edge.astype(jnp.int32))

    def tell(n):
        for d in (1 << n, -(1 << n)):
            pl.semaphore_signal(known.at[n], inc=1, device_id=on_z_at(d), device_id_type=MESH)

    def heard(n):
        pl.semaphore_wait(known.at[n], 2)


    def border(n):
        edge = zl // 7
        low = (3 - n) * edge + (4 + n) * (1 - edge)
        return remote(own_w, wb.at[1, outer, rows128(inner), :], m_send.at[n], m_recv, on_z(1 - zh, low))

    @pl.when(is_edge)
    def _():
        for n in range(4):
            border(n).start()

    def border_sent():
        @pl.when(is_edge)
        def _():
            for n in range(4):
                border(n).wait_send()

    opened(border_sent, (m_send,))
    opened(first_w, (m_recv,))

    def piece(h, o, d):
        return wb.at[h, o, rows128((inner - d + 4) % 4), :]

    def spread_inner(h, src):
        for d in (2, 1, 3):
            send(src, piece(h, outer, 0), (w_send, h, d - 1), (w_recv, h, d - 1), on_inner((inner + d) % 4))

    def spread_outer(h, d, src):
        to = piece(h, outer, d)
        send(src, to, (p2_send, h, d, 0), (p2_recv, h, d, 0), on_outer(right))
        send(src, to, (p2_send, h, d, 1), (p2_recv, h, d, 1), on_outer(left))

    def pass_on(h, d):
        arrived(piece(h, outer, d), (w_recv, h, d - 1))
        spread_outer(h, d, piece(h, outer, d))

    def relay(h, d):
        first = ((inner - d + 4) % 4) * 128
        arrived(piece(h, left, d), (p2_recv, h, d, 0))
        half = wb.at[h, left, pl.ds(pl.multiple_of(first, 128), 64), :]
        send(half, half, (p2_send, h, d, 2), (p2_recv, h, d, 2), on_outer(right))
        arrived(piece(h, right, d), (p2_recv, h, d, 1))
        half = wb.at[h, right, pl.ds(pl.multiple_of(first + 64, 64), 64), :]
        send(half, half, (p2_send, h, d, 3), (p2_recv, h, d, 3), on_outer(left))

    def relayed(h, d):
        first = ((inner - d + 4) % 4) * 128
        arrived(wb.at[h, across, pl.ds(pl.multiple_of(first, 128), 64), :], (p2_recv, h, d, 2))
        arrived(wb.at[h, across, pl.ds(pl.multiple_of(first + 64, 64), 64), :], (p2_recv, h, d, 3))

    spread_inner(0, own_w)
    spread_outer(0, 0, own_w)
    tell(0)

    def send_x(n, _):
        k, to, frm = x_columns(n, 1 - core)
        remote(
            x_ref.at[:, frm], xb.at[k, pl.ds(128, 128), to], x_send, x_recv, partner
        ).start()
        return 0

    lax.fori_loop(0, 32, send_x, 0)
    opened(half_x, (x_send,))
    opened(half_x, (x_recv,))

    def add_block(h, o):
        part[...] += dot(xb[h * 4 + o], wb[h, o])

    def turn(h, o):
        xt[h * 4 + o] = xb[h * 4 + o].T

    part[...] = jnp.zeros_like(part)
    arrived(qv, (local, 1))
    arrived(gv, (local, 2))
    arrived(segv, (local, 3))
    across_lanes = jnp.broadcast_to(segv[...], (128, 128))
    same = across_lanes.T == across_lanes
    row = lax.broadcasted_iota(jnp.int32, (128, 128), 0)
    column = lax.broadcasted_iota(jnp.int32, (128, 128), 1)
    mask[...] = jnp.where(same & (row <= column), 0.0, -1e30)

    for d in (1, 3, 2):
        pass_on(0, d)
    heard(0)
    tell(1)
    for d in (0, 1, 3):
        relay(0, d)
    arrived(piece(1, outer, 0), (m_recv,))
    spread_inner(1, piece(1, outer, 0))
    spread_outer(1, 0, piece(1, outer, 0))
    relay(0, 2)
    heard(1)
    tell(2)
    arrived(first_w, (local, 0))
    arrived(half_x, (local, 4))
    arrived(half_x, (x_recv,))
    add_block(0, outer)
    turn(0, outer)
    for d in (1, 3, 2):
        pass_on(1, d)
    add_block(0, left)
    add_block(0, right)
    turn(0, left)
    turn(0, right)
    for d in range(4):
        relayed(0, d)
    relay(1, 0)
    add_block(0, across)
    turn(0, across)
    relay(1, 1)
    relay(1, 3)
    add_block(1, outer)
    turn(1, outer)
    relay(1, 2)
    add_block(1, left)
    add_block(1, right)
    turn(1, left)
    turn(1, right)
    turn(1, across)
    for d in range(4):
        relayed(1, d)
    add_block(1, across)

    send(part.at[pl.ds(128, 128), :], part_in, (c_send, 0), (c_recv, 0), partner)
    arrived(part_in, (c_recv, 0))
    keyval = (part[pl.ds(0, 128), :] + part_in[...]).astype(BF16)
    keys, values = keyval[:, :HEAD], keyval[:, HEAD:]

    d_keys = jnp.zeros((128, HEAD), F32)
    d_values = jnp.zeros((128, HEAD), F32)
    for n in range(QH):
        cols = pl.ds(n * HEAD, HEAD)
        q, g = qv[:, cols], gv[:, cols]
        scores = dot_nt(keys, q) * SCALE + mask[...]
        weights = jnp.exp(scores - jnp.max(scores, axis=0, keepdims=True))
        probs = weights * (1.0 / jnp.sum(weights, axis=0, keepdims=True))
        d_probs = dot_nt(values, g)
        low = probs.astype(BF16)
        delta = jnp.sum(low.astype(F32) * d_probs, axis=0, keepdims=True)
        d_score = (probs * (d_probs - delta)).astype(BF16)
        dst[:, cols] = d_score
        d_keys += dot(d_score, q)
        d_values += dot(low, g)
    dkv[pl.ds(0, 128), pl.ds(0, HEAD)] = (d_keys * SCALE).astype(BF16)
    dkv[pl.ds(0, 128), pl.ds(HEAD, HEAD)] = d_values.astype(BF16)
    send(dkv.at[pl.ds(0, 128), :], dkv.at[pl.ds(128, 128), :], (c_send, 1), (c_recv, 1), partner)

    for n in range(QH):
        cols = pl.ds(n * HEAD, HEAD)
        dqv[:, cols] = (dot_tn(dst[:, cols], keys) * SCALE).astype(BF16)
    copy_here(dqv, dq_ref, (local, 5))
    arrived(dkv.at[pl.ds(128, 128), :], (c_recv, 1))

    heard(2)

    def term(h, o, d):
        return dot(xt[h * 4 + o, rows128((inner + d) % 4), :], dkv[...])

    def send_far(h, d):
        far[h, d] = term(h, across, d).astype(BF16)
        send(far.at[h, d, pl.ds(0, 64), :], far_l.at[h, d], (r1_send, h, d, 0), (r1_recv, h, d, 0), on_outer(right))
        send(far.at[h, d, pl.ds(64, 64), :], far_r.at[h, d], (r1_send, h, d, 1), (r1_recv, h, d, 1), on_outer(left))

    def send_joined(h, d):
        to_right, to_left = term(h, right, d), term(h, left, d)
        arrived(far_l.at[h, d], (r1_recv, h, d, 0))
        joined[h, d, 0, pl.ds(0, 64), :] = (to_right[:64] + far_l[h, d].astype(F32)).astype(BF16)
        joined[h, d, 0, pl.ds(64, 64), :] = to_right[64:].astype(BF16)
        send(joined.at[h, d, 0], in_l.at[h, d], (r1_send, h, d, 2), (r1_recv, h, d, 2), on_outer(right))
        arrived(far_r.at[h, d], (r1_recv, h, d, 1))
        joined[h, d, 1, pl.ds(0, 64), :] = to_left[:64].astype(BF16)
        joined[h, d, 1, pl.ds(64, 64), :] = (to_left[64:] + far_r[h, d].astype(F32)).astype(BF16)
        send(joined.at[h, d, 1], in_r.at[h, d], (r1_send, h, d, 3), (r1_recv, h, d, 3), on_outer(left))

    def input_grad(h, o):
        k = h * 4 + o
        di[k] = dot_nt(dkv[...], wb[h, o]).astype(BF16)

    def store_dx(n, _):
        k, frm, to = x_columns(n, core)
        pltpu.make_async_copy(
            di.at[k, pl.ds(0, 128), frm], dx_ref.at[:, to], local.at[6 + n // 16]
        ).start()
        remote(
            di.at[k, pl.ds(128, 128), frm], dx_ref.at[:, to], dx_send.at[n // 16], dx_recv.at[n // 16], partner
        ).start()
        return 0

    def write_dx(h):
        lax.fori_loop(h * 16, h * 16 + 16, store_dx, 0)
        quarter = xb.at[pl.ds(0, 2)]
        for sem in ((local, 6 + h), (dx_send, h), (dx_recv, h)):
            opened(quarter, sem)

    def outer_sum(h, d):
        total = term(h, outer, d)
        arrived(in_l.at[h, d], (r1_recv, h, d, 2))
        total += in_l[h, d].astype(F32)
        arrived(in_r.at[h, d], (r1_recv, h, d, 3))
        return total + in_r[h, d].astype(F32)

    def inner_ring(h, d):
        inner_out[h, d - 1] = outer_sum(h, d).astype(BF16)
        send(inner_out.at[h, d - 1], inner_in.at[h, d - 1], (r2_send, h, d - 1),
             (r2_recv, h, d - 1), on_inner((inner + d) % 4))

    def plane_sum(h):
        total = outer_sum(h, 0)
        for d in (2, 1, 3):
            arrived(inner_in.at[h, d - 1], (r2_recv, h, d - 1))
            total += inner_in[h, d - 1].astype(F32)
        z_out[h] = total.astype(BF16)
        for d in range(8):
            if h == 0 and d == 0:
                continue
            low = (zl + d) % 8
            rows = pl.ds(pl.multiple_of(low * 16, 16), 16)
            slot = h * 8 + d
            send(z_out.at[h, rows, :], z_in.at[slot], (z_send, slot), (z_recv, slot),
                 on_z((zh + h) % 2, low))

    away = [(1, 2), (1, 1), (1, 3), (0, 2), (0, 1), (0, 3)]
    for h, d in away + [(1, 0), (0, 0)]:
        send_far(h, d)
    for h, d in away + [(1, 0), (0, 0)]:
        send_joined(h, d)
    for h, d in away:
        inner_ring(h, d)
    plane_sum(1)
    plane_sum(0)
    for n in range(8):
        input_grad(n // 4, n % 4)
        if n % 4 == 3:
            write_dx(n // 4)

    mine = pl.ds(pl.multiple_of(zl * 16, 16), 16)
    total = z_out[0, mine, :].astype(F32)
    for slot in range(1, 16):
        arrived(z_in.at[slot], (z_recv, slot))
        total += z_in[slot].astype(F32)
    fin[mine, :] = total.astype(BF16)
    for d in range(1, 8):
        send(fin.at[mine, :], fin.at[mine, :], (f_send, d - 1), (f_recv, d - 1),
             on_z(zh, (zl + d) % 8))
    for d in range(1, 8):
        rows = pl.ds(pl.multiple_of(((zl - d + 8) % 8) * 16, 16), 16)
        arrived(fin.at[rows, :], (f_recv, d - 1))
    send(fin, fin_in, (c_send, 2), (c_recv, 2), partner)
    dwv[rows128(core), :] = fin[...].astype(F32)
    arrived(fin_in, (c_recv, 2))
    dwv[rows128(1 - core), :] = fin_in[...].astype(F32)
    copy_here(dwv, dw_ref, (local, 8))

    finish()


def store_kernel(a, b, c, a_out, b_out, c_out, sems):
    copies = [
        pltpu.make_async_copy(src, to, sems.at[n])
        for n, (src, to) in enumerate(((a, a_out), (b, b_out), (c, c_out)))
    ]
    for copy in copies:
        copy.start()
    for copy in copies:
        copy.wait()


def body(layer_input, queries, d_out, segment_ids, kv_weight):
    dma = pltpu.SemaphoreType.DMA
    any_space = pl.BlockSpec(memory_space=pl.ANY)
    shapes = (
        jax.ShapeDtypeStruct((128, 8192), BF16),
        jax.ShapeDtypeStruct((128, 512), BF16),
        jax.ShapeDtypeStruct((256, 256), F32),
    )
    results = pl.pallas_call(
        kernel,
        out_shape=shapes,
        in_specs=[pl.BlockSpec(memory_space=pltpu.HBM)] * 5,
        out_specs=(any_space,) * 3,
        scratch_shapes=[
            pltpu.VMEM((8, 256, 512), BF16),
            pltpu.VMEM((8, 512, 256), BF16),
            pltpu.VMEM((2, 4, 512, 256), BF16),
            pltpu.VMEM((128, 512), BF16),
            pltpu.VMEM((128, 512), BF16),
            pltpu.VMEM((1, 128), jnp.int32),
            pltpu.VMEM((128, 128), F32),
            pltpu.VMEM((256, 256), F32),
            pltpu.VMEM((128, 256), F32),
            pltpu.VMEM((128, 512), BF16),
            pltpu.VMEM((256, 256), BF16),
            pltpu.VMEM((8, 256, 512), BF16),
            pltpu.VMEM((128, 512), BF16),
            pltpu.VMEM((2, 4, 128, 256), BF16),
            pltpu.VMEM((2, 4, 2, 128, 256), BF16),
            pltpu.VMEM((2, 4, 64, 256), BF16),
            pltpu.VMEM((2, 4, 64, 256), BF16),
            pltpu.VMEM((2, 4, 128, 256), BF16),
            pltpu.VMEM((2, 4, 128, 256), BF16),
            pltpu.VMEM((2, 3, 128, 256), BF16),
            pltpu.VMEM((2, 3, 128, 256), BF16),
            pltpu.VMEM((2, 128, 256), BF16),
            pltpu.VMEM((16, 16, 256), BF16),
            pltpu.VMEM((128, 256), BF16),
            pltpu.VMEM((128, 256), BF16),
            pltpu.VMEM((256, 256), F32),
            dma((9,)),
            dma(()),
            dma(()),
            dma((2, 3)),
            dma((2, 3)),
            dma((2, 4, 4)),
            dma((2, 4, 4)),
            dma((4,)),
            dma(()),
            dma((3,)),
            dma((3,)),
            dma((2,)),
            dma((2,)),
            dma((2, 4, 4)),
            dma((2, 4, 4)),
            dma((2, 3)),
            dma((2, 3)),
            dma((16,)),
            dma((16,)),
            dma((7,)),
            dma((7,)),
            pltpu.SemaphoreType.REGULAR((3,)),
        ],
        compiler_params=pltpu.CompilerParams(
            collective_id=0, has_side_effects=True, vmem_limit_bytes=40 * 1024 * 1024
        ),
    )(*[
        pltpu.with_memory_space_constraint(a, pltpu.HBM)
        for a in (layer_input, queries, d_out, segment_ids, kv_weight)
    ])
    return pl.pallas_call(
        store_kernel,
        out_shape=shapes,
        in_specs=[any_space] * 3,
        out_specs=(any_space,) * 3,
        scratch_shapes=[dma((3,))],
        compiler_params=pltpu.CompilerParams(vmem_limit_bytes=4 * 1024 * 1024),
    )(*results)


def solution(mesh):
    return jax.shard_map(
        body,
        mesh=mesh,
        in_specs=(
            P(("rep", "shard"), None),
            P(("rep", "shard"), None),
            P(("rep", "shard"), None),
            P(("rep", "shard"), None),
            P("shard", None),
        ),
        out_specs=(P(("rep", "shard"), None), P(("rep", "shard"), None), P("shard", None)),
        check_vma=False,
    )
```

time: 88.7 us -> 76.2 us (0.86)
  local copies, waits for them, and re-layouts: 7.63 us -> 0 us
  Pallas kernels: 80.2 us -> 75.5 us
    unnamed x13 -> x0, local copies, waits for them, and re-layouts: 7.63 us -> none
    pallas_call x1 -> x2, Pallas kernels: 80.2 us -> 75.5 us  [the longest x1 74 us: body(): pl.pallas_call(kernel, out_shape=shapes, in_specs=[pl.BlockSpec(memory_sp...]
where the time goes in v2:
time: 76.2 us; the launch traced here: 76.1 us
  Pallas kernels  75.5 us (99%)
    pallas_call x1, Pallas kernels, body(): pl.pallas_call(kernel, out_shape=shapes, in_specs=[pl.BlockSpec(memory_sp...  74 us

profile of v2, /device:TPU:1, one launch (start us, length us, event | category | flops | bytes accessed | tf_op | source)
XLA Modules:
  0.0 76.1 jit_solution(12965387071287131238)
XLA Ops:
  0.6 74.0 %shard_map.76 = (bf16[128,8192]{1,0:T(8,128)(2,1)S(1)}, bf16[128,512]{1,0:T(8,128)(2,1)S(1)}, f32[256,256]{1,0:T(8,128)S(1)}) custom-call(bf16[128,8192]{1,0:T(8,128)(2,1)} %x_ref.1, bf16[128,512]{1,0:T(8,128)(2,1)} %q_ref.1, bf16[128,512]{1,0:T(8,128)(2,1)} %g_ref.1, s32[1,128]{1,0:T(1,128)} %seg_ref.1, bf16[256,256]{1,0:T(8,128)(2,1)} %w_ref.1), custom_call_target="tpu_custom_call" | custom-call | tf_op jit(solution)/shard_map/pallas_call | solution.py:425
  74.6 1.5 %shard_map.77 = (bf16[128,8192]{1,0:T(8,128)(2,1)}, bf16[128,512]{1,0:T(8,128)(2,1)}, f32[256,256]{1,0:T(8,128)}) custom-call(bf16[128,8192]{1,0:T(8,128)(2,1)S(1)} %get-tuple-element.6.a, bf16[128,512]{1,0:T(8,128)(2,1)S(1)} %get-tuple-element.7.b, f32[256,256]{1,0:T(8,128)S(1)} %get-tuple-element.8.c), custom_call_target="tpu_custom_call" | custom-call | tf_op jit(solution)/shard_map/pallas_call | solution.py:487

commit v3 on v2

--- a/solution.py
+++ b/solution.py
@@ -34,9 +34,9 @@
 def kernel(
     x_ref, q_ref, g_ref, seg_ref, w_ref,
     dx_ref, dq_ref, dw_ref,
-    xb, xt, wb, qv, gv, segv, mask, part, part_in, dst, dkv, di, dqv,
+    xb, wb, qv, gv, segv, mask, part, part_in, dst, dkv, di,
     far, joined, far_l, far_r, in_l, in_r,
-    inner_out, inner_in, z_out, z_in, fin, fin_in, dwv,
+    inner_out, inner_in, z_out, z_in, fin,
     local, x_send, x_recv, w_send, w_recv, p2_send, p2_recv, m_send, m_recv,
     c_send, c_recv, dx_send, dx_recv, r1_send, r1_recv, r2_send, r2_recv,
     z_send, z_recv, f_send, f_recv, known,
@@ -44,6 +44,7 @@
     rep, shard = lax.axis_index("rep"), lax.axis_index("shard")
     core, zl = rep % 2, rep // 2
     zh, y, x = shard // 16, (shard // 4) % 4, shard % 4
+    z = zh * 8 + zl
     outer = y * (1 - core) + x * core
     inner = x * (1 - core) + y * core
     right, left, across = (outer + 1) % 4, (outer + 3) % 4, (outer + 2) % 4
@@ -61,8 +62,8 @@
     is_edge = (zl == 0) | (zl == 7)
 
     def on_z_at(d):
-        z = (zh * 8 + zl + d + 16) % 16
-        return on_z(z // 8, z % 8)
+        there = (z + d + 16) % 16
+        return on_z(there // 8, there % 8)
 
 
     def rows128(i):
@@ -136,8 +137,6 @@
         return 0
 
     half_x = xb.at[pl.ds(0, 4)]
-    lax.fori_loop(0, 32, load_x, 0)
-    opened(half_x, (local, 4))
     pl.semaphore_wait(barrier, near + 4 * is_edge.astype(jnp.int32))
 
     def tell(n):
@@ -208,15 +207,14 @@
         ).start()
         return 0
 
+    lax.fori_loop(0, 32, load_x, 0)
+    opened(half_x, (local, 4))
     lax.fori_loop(0, 32, send_x, 0)
     opened(half_x, (x_send,))
     opened(half_x, (x_recv,))
 
     def add_block(h, o):
         part[...] += dot(xb[h * 4 + o], wb[h, o])
-
-    def turn(h, o):
-        xt[h * 4 + o] = xb[h * 4 + o].T
 
     part[...] = jnp.zeros_like(part)
     arrived(qv, (local, 1))
@@ -244,28 +242,20 @@
     arrived(half_x, (local, 4))
     arrived(half_x, (x_recv,))
     add_block(0, outer)
-    turn(0, outer)
-    for d in (1, 3, 2):
-        pass_on(1, d)
     add_block(0, left)
     add_block(0, right)
-    turn(0, left)
-    turn(0, right)
+    for d in (1, 3):
+        pass_on(1, d)
+    relay(1, 0)
+    pass_on(1, 2)
     for d in range(4):
         relayed(0, d)
-    relay(1, 0)
     add_block(0, across)
-    turn(0, across)
-    relay(1, 1)
-    relay(1, 3)
+    for d in (1, 3, 2):
+        relay(1, d)
     add_block(1, outer)
-    turn(1, outer)
-    relay(1, 2)
     add_block(1, left)
     add_block(1, right)
-    turn(1, left)
-    turn(1, right)
-    turn(1, across)
     for d in range(4):
         relayed(1, d)
     add_block(1, across)
@@ -296,14 +286,13 @@
 
     for n in range(QH):
         cols = pl.ds(n * HEAD, HEAD)
-        dqv[:, cols] = (dot_tn(dst[:, cols], keys) * SCALE).astype(BF16)
-    copy_here(dqv, dq_ref, (local, 5))
+        dq_ref[:, cols] = (dot_tn(dst[:, cols], keys) * SCALE).astype(BF16)
     arrived(dkv.at[pl.ds(128, 128), :], (c_recv, 1))
 
     heard(2)
 
     def term(h, o, d):
-        return dot(xt[h * 4 + o, rows128((inner + d) % 4), :], dkv[...])
+        return dot_tn(xb[((h + zh) % 2) * 4 + o, :, rows128((inner + d) % 4)], dkv[...])
 
     def send_far(h, d):
         far[h, d] = term(h, across, d).astype(BF16)
@@ -359,46 +348,62 @@
             arrived(inner_in.at[h, d - 1], (r2_recv, h, d - 1))
             total += inner_in[h, d - 1].astype(F32)
         z_out[h] = total.astype(BF16)
-        for d in range(8):
-            if h == 0 and d == 0:
-                continue
-            low = (zl + d) % 8
-            rows = pl.ds(pl.multiple_of(low * 16, 16), 16)
-            slot = h * 8 + d
-            send(z_out.at[h, rows, :], z_in.at[slot], (z_send, slot), (z_recv, slot),
-                 on_z((zh + h) % 2, low))
-
-    away = [(1, 2), (1, 1), (1, 3), (0, 2), (0, 1), (0, 3)]
-    for h, d in away + [(1, 0), (0, 0)]:
+
+        def each(act):
+            for low in range(8):
+                ahead = (8 * h + low - z + 16) % 16
+
+                @pl.when(ahead != 0)
+                def _():
+                    act(remote(z_out.at[h, pl.ds(low * 16, 16), :], z_in.at[ahead],
+                               z_send.at[h, low], z_recv.at[ahead], on_z(h, low)))
+
+        each(lambda copy: copy.start())
+        opened(lambda: each(lambda copy: copy.wait_send()), (z_send, h))
+
+    order = [(h, d) for h in (0, 1) for d in (2, 1, 3, 0)]
+    for h, d in order:
         send_far(h, d)
-    for h, d in away + [(1, 0), (0, 0)]:
+    for h, d in order:
         send_joined(h, d)
-    for h, d in away:
-        inner_ring(h, d)
+    for d in (2, 1, 3):
+        inner_ring(0, d)
+    inner_ring(1, 2)
+    inner_ring(1, 1)
+    plane_sum(0)
+    inner_ring(1, 3)
     plane_sum(1)
-    plane_sum(0)
     for n in range(8):
         input_grad(n // 4, n % 4)
         if n % 4 == 3:
             write_dx(n // 4)
 
-    mine = pl.ds(pl.multiple_of(zl * 16, 16), 16)
-    total = z_out[0, mine, :].astype(F32)
-    for slot in range(1, 16):
-        arrived(z_in.at[slot], (z_recv, slot))
-        total += z_in[slot].astype(F32)
+    def owned(low, at_core):
+        return pl.ds(pl.multiple_of(at_core * 128 + low * 16, 16), 16)
+
+    mine = owned(zl, core)
+    total = z_out[zh, pl.ds(pl.multiple_of(zl * 16, 16), 16), :].astype(F32)
+    for ahead in range(1, 16):
+        pltpu.make_async_copy(z_in.at[ahead], z_in.at[ahead], z_recv.at[ahead]).wait()
+        total += z_in[ahead].astype(F32)
     fin[mine, :] = total.astype(BF16)
-    for d in range(1, 8):
-        send(fin.at[mine, :], fin.at[mine, :], (f_send, d - 1), (f_recv, d - 1),
-             on_z(zh, (zl + d) % 8))
-    for d in range(1, 8):
-        rows = pl.ds(pl.multiple_of(((zl - d + 8) % 8) * 16, 16), 16)
-        arrived(fin.at[rows, :], (f_recv, d - 1))
-    send(fin, fin_in, (c_send, 2), (c_recv, 2), partner)
-    dwv[rows128(core), :] = fin[...].astype(F32)
-    arrived(fin_in, (c_recv, 2))
-    dwv[rows128(1 - core), :] = fin_in[...].astype(F32)
-    copy_here(dwv, dw_ref, (local, 8))
+    for n in range(7):
+        low = n + (n >= zl).astype(jnp.int32)
+        for other in (0, 1):
+            at_core = core * (1 - other) + (1 - core) * other
+            remote(fin.at[mine, :], fin.at[mine, :], f_send.at[other, n], f_recv.at[other, zl],
+                   (low * 2 + at_core, shard)).start()
+            opened(fin.at[mine, :], (f_send, other, n))
+    send(fin.at[mine, :], fin.at[mine, :], (c_send, 2), (c_recv, 2), partner)
+    arrived(fin.at[owned(zl, 1 - core), :], (c_recv, 2))
+    for other in (0, 1):
+        at_core = core * (1 - other) + (1 - core) * other
+        for d in range(1, 8):
+            low = (zl + d) % 8
+            pltpu.make_async_copy(
+                fin.at[owned(low, at_core), :], fin.at[owned(low, at_core), :], f_recv.at[other, low]
+            ).wait()
+    dw_ref[...] = fin[...].astype(F32)
 
     finish()
 
@@ -426,10 +431,9 @@
         kernel,
         out_shape=shapes,
         in_specs=[pl.BlockSpec(memory_space=pltpu.HBM)] * 5,
-        out_specs=(any_space,) * 3,
+        out_specs=(any_space,) + (pl.BlockSpec(memory_space=pltpu.VMEM),) * 2,
         scratch_shapes=[
             pltpu.VMEM((8, 256, 512), BF16),
-            pltpu.VMEM((8, 512, 256), BF16),
             pltpu.VMEM((2, 4, 512, 256), BF16),
             pltpu.VMEM((128, 512), BF16),
             pltpu.VMEM((128, 512), BF16),
@@ -440,7 +444,6 @@
             pltpu.VMEM((128, 512), BF16),
             pltpu.VMEM((256, 256), BF16),
             pltpu.VMEM((8, 256, 512), BF16),
-            pltpu.VMEM((128, 512), BF16),
             pltpu.VMEM((2, 4, 128, 256), BF16),
             pltpu.VMEM((2, 4, 2, 128, 256), BF16),
             pltpu.VMEM((2, 4, 64, 256), BF16),
@@ -451,9 +454,7 @@
             pltpu.VMEM((2, 3, 128, 256), BF16),
             pltpu.VMEM((2, 128, 256), BF16),
             pltpu.VMEM((16, 16, 256), BF16),
-            pltpu.VMEM((128, 256), BF16),
-            pltpu.VMEM((128, 256), BF16),
-            pltpu.VMEM((256, 256), F32),
+            pltpu.VMEM((256, 256), BF16),
             dma((9,)),
             dma(()),
             dma(()),
@@ -471,10 +472,10 @@
             dma((2, 4, 4)),
             dma((2, 3)),
             dma((2, 3)),
+            dma((2, 8)),
             dma((16,)),
-            dma((16,)),
-            dma((7,)),
-            dma((7,)),
+            dma((2, 7)),
+            dma((2, 8)),
             pltpu.SemaphoreType.REGULAR((3,)),
         ],
         compiler_params=pltpu.CompilerParams(

time: 76.2 us -> 73.1 us (0.959)
  Pallas kernels: 75.5 us -> 72.3 us
    pallas_call x1, Pallas kernels: 74 us -> 70.9 us  [body(): pl.pallas_call(kernel, out_shape=shapes, in_specs=[pl.BlockSpec(memory_sp...]
where the time goes in v3:
time: 73.1 us; the launch traced here: 73 us
  Pallas kernels  72.3 us (99%)
    pallas_call x1, Pallas kernels, body(): pl.pallas_call(kernel, out_shape=shapes, in_specs=[pl.BlockSpec(memory_sp...  70.9 us
    pallas_call x1, Pallas kernels, body(): pl.pallas_call(store_kernel, out_shape=shapes, in_specs=[any_space] * 3,...  1.46 us

profile of v3, /device:TPU:1, one launch (start us, length us, event | category | flops | bytes accessed | tf_op | source)
XLA Modules:
  0.0 73.0 jit_solution(14615982419696120390)
XLA Ops:
  0.6 70.9 %shard_map.76 = (bf16[128,8192]{1,0:T(8,128)(2,1)S(1)}, bf16[128,512]{1,0:T(8,128)(2,1)S(1)}, f32[256,256]{1,0:T(8,128)S(1)}) custom-call(bf16[128,8192]{1,0:T(8,128)(2,1)} %x_ref.1, bf16[128,512]{1,0:T(8,128)(2,1)} %q_ref.1, bf16[128,512]{1,0:T(8,128)(2,1)} %g_ref.1, s32[1,128]{1,0:T(1,128)} %seg_ref.1, bf16[256,256]{1,0:T(8,128)(2,1)} %w_ref.1), custom_call_target="tpu_custom_call" | custom-call | tf_op jit(solution)/shard_map/pallas_call | solution.py:430
  71.5 1.5 %shard_map.77 = (bf16[128,8192]{1,0:T(8,128)(2,1)}, bf16[128,512]{1,0:T(8,128)(2,1)}, f32[256,256]{1,0:T(8,128)}) custom-call(bf16[128,8192]{1,0:T(8,128)(2,1)S(1)} %get-tuple-element.6.a, bf16[128,512]{1,0:T(8,128)(2,1)S(1)} %get-tuple-element.7.b, f32[256,256]{1,0:T(8,128)S(1)} %get-tuple-element.8.c), custom_call_target="tpu_custom_call" | custom-call | tf_op jit(solution)/shard_map/pallas_call | solution.py:488

commit v4 on v3

--- a/solution.py
+++ b/solution.py
@@ -373,10 +373,9 @@
     plane_sum(0)
     inner_ring(1, 3)
     plane_sum(1)
-    for n in range(8):
-        input_grad(n // 4, n % 4)
-        if n % 4 == 3:
-            write_dx(n // 4)
+    for n in range(4):
+        input_grad(0, n)
+    write_dx(0)
 
     def owned(low, at_core):
         return pl.ds(pl.multiple_of(at_core * 128 + low * 16, 16), 16)
@@ -395,6 +394,9 @@
                    (low * 2 + at_core, shard)).start()
             opened(fin.at[mine, :], (f_send, other, n))
     send(fin.at[mine, :], fin.at[mine, :], (c_send, 2), (c_recv, 2), partner)
+    for n in range(4):
+        input_grad(1, n)
+    write_dx(1)
     arrived(fin.at[owned(zl, 1 - core), :], (c_recv, 2))
     for other in (0, 1):
         at_core = core * (1 - other) + (1 - core) * other

time: 73.1 us -> 73.1 us (level)
  no operation moved by 1% of the time
where the time goes in v4:
time: 73.1 us; the launch traced here: 73 us
  Pallas kernels  72.3 us (99%)
    pallas_call x1, Pallas kernels, body(): pl.pallas_call(kernel, out_shape=shapes, in_specs=[pl.BlockSpec(memory_sp...  70.9 us
    pallas_call x1, Pallas kernels, body(): pl.pallas_call(store_kernel, out_shape=shapes, in_specs=[any_space] * 3,...  1.46 us

profile of v4, /device:TPU:1, one launch (start us, length us, event | category | flops | bytes accessed | tf_op | source)
XLA Modules:
  0.0 73.0 jit_solution(5765206089685865440)
XLA Ops:
  0.6 70.9 %shard_map.76 = (bf16[128,8192]{1,0:T(8,128)(2,1)S(1)}, bf16[128,512]{1,0:T(8,128)(2,1)S(1)}, f32[256,256]{1,0:T(8,128)S(1)}) custom-call(bf16[128,8192]{1,0:T(8,128)(2,1)} %x_ref.1, bf16[128,512]{1,0:T(8,128)(2,1)} %q_ref.1, bf16[128,512]{1,0:T(8,128)(2,1)} %g_ref.1, s32[1,128]{1,0:T(1,128)} %seg_ref.1, bf16[256,256]{1,0:T(8,128)(2,1)} %w_ref.1), custom_call_target="tpu_custom_call" | custom-call | tf_op jit(solution)/shard_map/pallas_call | solution.py:432
  71.5 1.5 %shard_map.77 = (bf16[128,8192]{1,0:T(8,128)(2,1)}, bf16[128,512]{1,0:T(8,128)(2,1)}, f32[256,256]{1,0:T(8,128)}) custom-call(bf16[128,8192]{1,0:T(8,128)(2,1)S(1)} %get-tuple-element.6.a, bf16[128,512]{1,0:T(8,128)(2,1)S(1)} %get-tuple-element.7.b, f32[256,256]{1,0:T(8,128)S(1)} %get-tuple-element.8.c), custom_call_target="tpu_custom_call" | custom-call | tf_op jit(solution)/shard_map/pallas_call | solution.py:490
